TPU v7x, 256 devices: a whole 4x4x8 slice. The times are simulated.
256 devices in a mesh: sample: 4 (over z_lo, core), row: 16 (over y, z_hi), col: 4 (over x).
Axes of the slice: x: 4, y: 4, z: 8 (z_hi: 4, z_lo: 2; z = z_hi * 2 + z_lo), core: 2. Of those that a mesh axis runs over, the one named last changes fastest.
Arguments:
- single: bfloat16 [16384, 384], P(('sample', 'row')), parts along dimension 0, may hold values from -16 to 16
- pair_bias: bfloat16 [64, 4096, 4096], P('sample', 'row', 'col'), parts along dimension 0, may hold values from -4 to 400
- token_mask: int32 [16384], P('sample'), parts along dimension 0, may hold values from 0 to 1, as said below
- norm_gain: float32 [384], replicated, may hold values from 0.25 to 1.75
- w_query: bfloat16 [384, 384], replicated, may hold values from -0.3125 to 0.3125
- query_bias: float32 [384], replicated, may hold values from -3 to 3
- w_key: bfloat16 [384, 384], replicated, may hold values from -0.3125 to 0.3125
- w_value: bfloat16 [384, 384], replicated, may hold values from -0.3125 to 0.3125
- w_gate: bfloat16 [384, 384], replicated, may hold values from -0.3125 to 0.3125
- w_out: bfloat16 [384, 384], P(None, 'col'), may hold values from -0.3125 to 0.3125
Outputs:
- updated: float32 [16384, 384], P(('sample', 'row'), 'col'), parts along dimension 0
There are 4 independent parts, one for each index of `sample`. A program takes and returns all parts, laid end to end along the dimension named above; an argument that names none is the same for every part. Nothing has to cross between parts.
Inputs may be any that keep to these rules, and one draw needn't show every extreme that they name: `token_mask`: 1 for a leading run of 512 or more tokens and 0 for every token after it.
All inputs are finite; a program needn't handle non-finite values.
Results may differ from a plain program's by a relative error of at most 0.0014.
Values may be sent and summed in bfloat16 or wider, within the bound.
A program may use at most 128 MiB of HBM per device.

v0:
```python
import math

import jax
import jax.numpy as jnp
from jax import lax
from jax.sharding import PartitionSpec as P

D = 384
HEADS = 16


def joined(array, axis, combine):
    everything = jax.tree.map(lambda part: lax.all_gather(part, axis), array)
    initial = jax.tree.map(lambda part: part[0], everything)

    def lap(k, so_far):
        return combine(so_far, jax.tree.map(lambda part: part[k], everything))

    return lax.fori_loop(1, lax.axis_size(axis), lap, initial)


def layer_norm(single, norm_gain):
    values_f32 = single.astype(jnp.float32)
    row_mean = jnp.mean(values_f32, axis=1, keepdims=True)
    centered = values_f32 - row_mean
    row_var = jnp.mean(centered * centered, axis=1, keepdims=True)
    return (centered * lax.rsqrt(row_var + 1e-05) * norm_gain).astype(jnp.bfloat16)


def attend(query_rows, key_rows, value_rows, bias_block, mask_cols):
    row_count = query_rows.shape[0]
    col_count = key_rows.shape[0]
    query_heads = query_rows.reshape(row_count, HEADS, -1)
    key_heads = key_rows.reshape(col_count, HEADS, -1)
    value_heads = value_rows.reshape(col_count, HEADS, -1)
    logits = jnp.einsum("qhd,khd->hqk", query_heads, key_heads, preferred_element_type=jnp.float32)
    mask_term = (mask_cols.astype(jnp.float32) - 1.0) * 1000000.0
    logits = logits + bias_block.astype(jnp.float32) + mask_term[None, None, :]
    row_peak = jnp.max(logits, axis=2)
    exp_scores = jnp.exp(logits - row_peak[:, :, None])
    row_total = jnp.sum(exp_scores, axis=2)
    weighted = jnp.einsum(
        "hqk,khd->qhd",
        exp_scores.astype(jnp.bfloat16),
        value_heads,
        preferred_element_type=jnp.float32,
    )
    return (row_peak.T, row_total.T, weighted.reshape(row_count, -1))


def combine(first, second):
    peak_one, total_one, weighted_one = first
    peak_two, total_two, weighted_two = second
    row_peak = jnp.maximum(peak_one, peak_two)
    factor_one = jnp.exp(peak_one - row_peak)
    factor_two = jnp.exp(peak_two - row_peak)
    width_head = weighted_one.shape[1] // peak_one.shape[1]
    row_total = total_one * factor_one + total_two * factor_two
    weighted = weighted_one * jnp.repeat(
        factor_one, width_head, axis=1
    ) + weighted_two * jnp.repeat(factor_two, width_head, axis=1)
    return (row_peak, row_total, weighted)


def on_device(
    single, pair_bias, token_mask, norm_gain, w_query, query_bias, w_key, w_value, w_gate, w_out
):
    head_dim = D // HEADS
    inv_sqrt = 1.0 / math.sqrt(head_dim)
    tokens = token_mask.shape[0]
    col_total = lax.axis_size("col")
    col_tokens = tokens // col_total
    out_width = w_out.shape[1]
    col_pos = lax.axis_index("col")
    normed = layer_norm(single, norm_gain)
    query = (
        (jnp.dot(normed, w_query, preferred_element_type=jnp.float32) + query_bias) * inv_sqrt
    ).astype(jnp.bfloat16)
    gate_act = jax.nn.sigmoid(jnp.dot(normed, w_gate, preferred_element_type=jnp.float32))
    single_cols = lax.dynamic_slice_in_dim(single, col_pos * out_width, out_width, 1).astype(
        jnp.float32
    )
    key_local = jnp.dot(normed, w_key, preferred_element_type=jnp.float32).astype(jnp.bfloat16)
    value_local = jnp.dot(normed, w_value, preferred_element_type=jnp.float32).astype(jnp.bfloat16)
    key_all, value_all = (
        lax.all_gather(key_local, "row", axis=0, tiled=True),
        lax.all_gather(value_local, "row", axis=0, tiled=True),
    )
    col_start = col_pos * col_tokens
    key_rows = lax.dynamic_slice_in_dim(key_all, col_start, col_tokens, 0)
    value_rows = lax.dynamic_slice_in_dim(value_all, col_start, col_tokens, 0)
    mask_cols = lax.dynamic_slice_in_dim(token_mask, col_start, col_tokens, 0)
    partial_value = attend(query, key_rows, value_rows, pair_bias, mask_cols)
    row_peak, row_total, weighted = joined(partial_value, "col", combine)
    attended = weighted / jnp.repeat(row_total, head_dim, axis=1)
    gated = (gate_act * attended).astype(jnp.bfloat16)
    result = single_cols + jnp.dot(gated, w_out, preferred_element_type=jnp.float32)
    return result


def solution(mesh):
    return jax.shard_map(
        on_device,
        mesh=mesh,
        in_specs=(
            P(("sample", "row"), None),
            P("sample", "row", "col"),
            P("sample"),
            P(),
            P(),
            P(),
            P(),
            P(),
            P(),
            P(None, "col"),
        ),
        out_specs=P(("sample", "row"), "col"),
        check_vma=False,
    )
```

profile of v0, /device:TPU:8, one launch (start us, length us, event | category | flops | bytes accessed | tf_op | source)
XLA Modules:
  0.0 213.2 jit_solution(2028157395418642976)
XLA Ops:
  6.5 0.0 copy-start
  6.5 0.0 all-gather.8.cloned.1.call-start
  6.5 1.1 convert_reduce_fusion
  7.6 1.1 fusion.20
  8.8 0.0 copy-done
  8.8 1.9 convolution_convert_fusion
  10.7 0.0 all-gather.8.cloned.1.call-update
  10.7 0.0 all-gather.6.cloned.1.call-start
  10.8 2.1 convolution_convert_fusion.1
  12.9 0.0 all-gather.6.cloned.1.call-update
  12.9 0.0 all-gather.10.cloned.1.call-start
  13.0 1.4 fusion.15
  14.4 0.1 copy.24
  14.5 0.7 add_multiply_fusion
  15.2 66.2 %all-gather.8.cloned.1.call-done = bf16[4096,384]{1,0:T(8,128)(2,1)} async-done(((bf16[256,384]{1,0:T(8,128)(2,1)}), bf16[4096,384]{1,0:T(8,128)(2,1)}) %all-gather.8.cloned.1.call-update) | async-done | bytes 3145744 | tf_op jit(solution)/shard_map/all_gather | solution.py:87
  81.4 68.2 %all-gather.6.cloned.1.call-done = bf16[4096,384]{1,0:T(8,128)(2,1)} async-done(((bf16[256,384]{1,0:T(8,128)(2,1)}), bf16[4096,384]{1,0:T(8,128)(2,1)}) %all-gather.6.cloned.1.call-update) | async-done | bytes 3145744 | tf_op jit(solution)/shard_map/all_gather | solution.py:86
  149.6 1.5 constant_dynamic-slice_fusion.3
  151.2 0.3 copy.25
  151.5 0.3 copy.26
  151.8 0.0 copy-start.2
  151.8 5.6 %fusion.32 = (f32[16,256]{1,0:T(8,128)S(1)}, f32[16,256,1024]{2,1,0:T(8,128)S(1)}) fusion(f32[1024]{0:T(1024)S(1)} %add_multiply_fusion, bf16[16,256,1024]{2,1,0:T(8,128)(2,1)} %param.13, bf16[256,16,24]{0,2,1:T(8,128)(2,1)S(1)} %bitcast.59, bf16[1024,16,24]{0,2,1:T(8,128)(2,1)S(1)} %bitcast.55), kind=kOutput, calls=%fused_computation.49 | convolution fusion | flops 218099712 | bytes 26169344 | tf_op jit(solution)/shard_map/qhd,khd->hqk/dot_general | solution.py:36
  157.4 0.0 copy-start.1
  157.4 5.7 %copy-done.1 = f32[16,256,1024]{2,1,0:T(8,128)} copy-done((f32[16,256,1024]{2,1,0:T(8,128)}, f32[16,256,1024]{2,1,0:T(8,128)S(1)}, u32[]{:S(2)}) %copy-start.1) | copy-done | bytes 16777240
  163.1 3.1 %fusion.6 = f32[16,24,256]{2,1,0:T(8,128)S(1)} fusion(bf16[1024,16,24]{0,2,1:T(8,128)(2,1)S(1)} %bitcast.56, f32[16,256,1024]{2,1,0:T(8,128)S(1)} %get-tuple-element.219, f32[16,256]{1,0:T(8,128)S(1)} %get-tuple-element.218), kind=kOutput, calls=%fused_computation.17 | convolution fusion | flops 209715200 | bytes 17973248 | tf_op jit(solution)/shard_map/hqk,khd->qhd/dot_general | solution.py:42
  166.2 0.9 copy.27
  167.1 0.0 all-gather.10.cloned.1.call-update
  167.1 0.0 copy-done.2
  167.2 0.1 constant_dynamic-slice_fusion.5
  167.3 0.1 copy.37
  167.4 12.2 %all-gather = f32[1024,16]{0,1:T(8,128)S(1)} all-gather(f32[256,16]{0,1:T(8,128)S(1)} %bitcast.60), channel_id=2, replica_groups=mesh['sample'=4,'row'=16,'col'=4] {'col'}, dimensions={0}, use_global_device_ids=true | all-gather | bytes 81920 | tf_op jit(solution)/shard_map/all_gather | solution.py:13
  179.6 0.0 copy-start.3
  179.6 0.0 copy-start.4
  179.6 0.0 copy-start.5
  179.6 7.8 %fusion.5 = f32[16,256]{1,0:T(8,128)S(1)} fusion(f32[16,256,1024]{2,1,0:T(8,128)} %copy-done.1, f32[16,256]{1,0:T(8,128)S(1)} %get-tuple-element.218), kind=kLoop, calls=%fused_computation.16 | loop fusion | flops 8384512 | bytes 16809984 | tf_op jit(solution)/shard_map/reduce_sum | solution.py:41
  187.4 12.0 %all-gather.1 = f32[1024,16]{0,1:T(8,128)S(1)} all-gather(f32[256,16]{0,1:T(8,128)S(1)} %bitcast.61), channel_id=3, replica_groups=mesh['sample'=4,'row'=16,'col'=4] {'col'}, dimensions={0}, use_global_device_ids=true | all-gather | bytes 81920 | tf_op jit(solution)/shard_map/all_gather | solution.py:13
  199.4 0.0 all-gather.10.cloned.1.call-done
  199.5 1.0 slice_bitcast_fusion
  200.5 0.2 copy.28
  200.7 4.4 %while.19 = (s32[]{:T(128)}, f32[256,16]{0,1:T(8,128)S(1)}, f32[256,16]{0,1:T(8,128)S(1)}, f32[256,384]{0,1:T(8,128)S(1)}, f32[4,256,16]{1,0,2:T(4,128)S(1)}, /*...) while((s32[]{:T(128)}, f32[256,16]{0,1:T(8,128)S(1)}, ...), condition=%wide.region_5.0_spmd, body=%wide.region_4.0_spmd.sunk | while | flops 319493 | bytes 2982039 | solution.py:19
  200.8 1.0 constant_dynamic-slice_fusion.9
  201.8 0.2 copy.53
  202.0 0.2 fusion.44
  202.2 1.0 constant_dynamic-slice_fusion.9
  203.2 0.2 copy.53
  203.4 0.2 fusion.44
  203.7 1.0 constant_dynamic-slice_fusion.9
  204.7 0.2 copy.53
  204.9 0.2 fusion.44
  205.1 0.2 copy.32
  205.3 0.2 copy.33
  205.4 0.0 copy-done.3
  205.4 0.0 copy-done.4
  205.4 0.0 copy-done.5
  205.5 1.2 fusion.17
  (13 shorter events, 0.3 us)
Async XLA Ops:
  6.5 2.2 %copy-start = (bf16[384,384]{1,0:T(8,128)(2,1)S(1)}, bf16[384,384]{1,0:T(8,128)(2,1)}, u32[]{:S(2)}) copy-start(bf16[384,384]{1,0:T(8,128)(2,1)} %param.19) | copy-start | bytes 884740
  6.5 74.9 %all-gather.8.cloned.1.call-start = ((), (), s32[]{:S(2)}) async-start(), calls=%async_computation.1 | async-start | bytes 3342336 | tf_op jit(solution)/shard_map/all_gather | solution.py:87
  10.7 138.9 %all-gather.6.cloned.1.call-start = ((), (), s32[]{:S(2)}) async-start(), calls=%async_computation | async-start | bytes 3342336 | tf_op jit(solution)/shard_map/all_gather | solution.py:86
  12.9 186.5 %all-gather.10.cloned.1.call-start = ((), (), s32[]{:S(2)}) async-start(), calls=%async_computation.2 | async-start | bytes 1966080 | tf_op jit(solution)/shard_map/all_gather | solution.py:13
  151.8 15.4 %copy-start.2 = (bf16[256,384]{1,0:T(8,128)(2,1)S(1)}, bf16[256,384]{1,0:T(8,128)(2,1)}, u32[]{:S(2)}) copy-start(bf16[256,384]{1,0:T(8,128)(2,1)} %param.12) | copy-start | bytes 589828
  157.4 5.7 %copy-start.1 = (f32[16,256,1024]{2,1,0:T(8,128)}, f32[16,256,1024]{2,1,0:T(8,128)S(1)}, u32[]{:S(2)}) copy-start(f32[16,256,1024]{2,1,0:T(8,128)S(1)} %get-tuple-element.219) | copy-start | bytes 50331652
  179.6 25.9 %copy-start.3 = (bf16[384,384]{1,0:T(8,128)(2,1)S(1)}, bf16[384,384]{1,0:T(8,128)(2,1)}, u32[]{:S(2)}) copy-start(bf16[384,384]{1,0:T(8,128)(2,1)} %param.20) | copy-start | bytes 884740
  179.6 25.9 %copy-start.4 = (bf16[384,96]{0,1:T(8,128)(2,1)S(1)}, bf16[384,96]{0,1:T(8,128)(2,1)}, u32[]{:S(2)}) copy-start(bf16[384,96]{0,1:T(8,128)(2,1)} %param.21) | copy-start | bytes 221188
  179.6 25.9 %copy-start.5 = (f32[384]{0:T(512)S(1)}, f32[384]{0:T(512)}, u32[]{:S(2)}) copy-start(f32[384]{0:T(512)} %param.15) | copy-start | bytes 4612
Sparse Core Ops, SparseCore 0:
  10.9 70.4 all-gather.7
  83.9 65.7 all-gather.5
  167.3 27.4 all-gather.9
where the time goes:
time: 214 us; the launch traced here: 213 us
  waiting for transfers between devices  134 us (63%)
  blocking collectives  24.2 us (11%)
  matrix products  15.3 us (7%)
  local copies, waits for them, and re-layouts  14.4 us (7%)
  between operations  13.3 us (6%)
  other arithmetic  11.2 us (5%)
    all_gather x1, waiting for transfers between devices, on_device(): lax.all_gather(key_local, 'row', axis=0, tiled=True)  68.2 us
    all_gather x1, waiting for transfers between devices, on_device(): lax.all_gather(value_local, 'row', axis=0, tiled=True)  66.2 us
    all_gather x2, blocking collectives, joined(): everything = jax.tree.map(lambda part: lax.all_gather(part, axis), array)  24.2 us
    reduce_sum x1, other arithmetic, attend(): row_total = jnp.sum(exp_scores, axis=2)  7.77 us
    unnamed x13, local copies, waits for them, and re-layouts  5.86 us
    dot_general x1, matrix products, attend(): jnp.einsum('qhd,khd->hqk', query_heads, key_heads, preferred_element_type...  5.59 us
  transfers between devices with their start and end apart: 3, of which 2 were waited for; matrix products, arithmetic and copies ran while one was open for 6% of the time, Pallas kernels for 0%

commit v1 on v0

v1 whole, which is shorter than its diff:
```python
import functools
import math

import jax
import jax.numpy as jnp
from jax import lax
from jax.experimental import pallas as pl
from jax.experimental.pallas import tpu as pltpu
from jax.sharding import PartitionSpec as P

D = 384
HEADS = 16
HD = 24
PAD = 32
WIDE = HEADS * PAD
GROUPS = 4
LANES = 128
ROWS = 256
PART = 64
OUTW = 96
MESH = pl.DeviceIdType.MESH
F32 = jnp.float32
BF16 = jnp.bfloat16
MASK_HI = 999424.0
MASK_LO = 576.0


def iota(shape, dim):
    return lax.broadcasted_iota(jnp.int32, shape, dim)


def mm(a, b):
    return lax.dot_general(a, b, (((1,), (0,)), ((), ())), preferred_element_type=F32)


def mm_nt(a, b):
    return lax.dot_general(a, b, (((1,), (1,)), ((), ())), preferred_element_type=F32)


def layer_norm(values, gain):
    values = values.astype(F32)
    centered = values - jnp.mean(values, axis=1, keepdims=True)
    var = jnp.mean(centered * centered, axis=1, keepdims=True)
    return (centered * lax.rsqrt(var + 1e-05) * gain).astype(BF16)


def spread_matrix(first):
    def make(width):
        src, dst = iota((D, width), 0), iota((D, width), 1)
        hit = (src == (dst // PAD + first) * HD + dst % PAD) & (dst % PAD < HD)
        return jnp.where(hit, 1.0, 0.0).astype(BF16)

    return make


def kernel(
    single, bias, mask, gain, w_query, q_bias, w_key, w_value, w_gate, w_out, out,
    s_v, b_v, mask_v, gain_v, qb_v, wq_v, wk_v, wv_v, wg_v, wo_v,
    ybuf, kbuf, qm, wkt, wvp, wop, gate_v, cols_v, kt, vm, p4, mrun, acc, part, got, gbuf,
    lsem, bsem, zs, zr, ys, yr, xs, xr, ps, pr, gs, gr,
):
    col = lax.axis_index("col")
    row = lax.axis_index("row")
    x, y, z = col, row // 4, row % 4

    def dev(cx, cy, cz):
        return {"row": cy * 4 + cz, "col": cx}

    def rdma(src, dst, ssem, rsem, target):
        return pltpu.make_async_remote_copy(
            src_ref=src, dst_ref=dst, send_sem=ssem, recv_sem=rsem,
            device_id=target, device_id_type=MESH,
        )

    tokens = 4 * ROWS
    loads = [
        (single, s_v), (gain, gain_v), (q_bias, qb_v), (w_query, wq_v), (w_key, wk_v),
        (w_value, wv_v), (w_gate, wg_v), (w_out, wo_v),
        (mask.at[pl.ds(pl.multiple_of(col * tokens, tokens), tokens)], mask_v),
    ]
    loads = [pltpu.make_async_copy(a, b, lsem.at[i]) for i, (a, b) in enumerate(loads)]
    for load in loads:
        load.start()

    def chunk_cols(d):
        return pl.ds(pl.multiple_of(((z + d) % 4) * ROWS, ROWS), ROWS)

    order = (0, 1, 3, 2)

    def bias_load(d):
        return pltpu.make_async_copy(bias.at[:, :, chunk_cols(d)], b_v.at[d], bsem.at[d])

    barrier = pltpu.get_barrier_semaphore()
    peers = [dev((x + k) % 4, y, z) for k in (1, 2, 3)]
    peers += [dev(x, (y + k) % 4, z) for k in (1, 2, 3)]
    peers += [dev(x, y, (z + k) % 4) for k in (1, 2, 3)]
    for peer in peers:
        pl.semaphore_signal(barrier, inc=1, device_id=peer, device_id_type=MESH)
    for d in order:
        bias_load(d).start()

    for load in loads:
        load.wait()
    pl.semaphore_wait(barrier, len(peers))

    diag = x == y
    mine = pl.ds(pl.multiple_of(x * PART, PART), PART)
    own = s_v.at[mine]

    def zc(d):
        return rdma(own, ybuf.at[y, d], zs.at[d], zr.at[d], dev(x, y, (z + 4 - d) % 4))

    def yc(d, k):
        return rdma(ybuf.at[y, d], ybuf.at[y, d], ys.at[d, k], yr.at[d, 4 - k], dev(x, (y + k) % 4, z))

    def yw(d, k):
        other = (y + k) % 4
        return rdma(ybuf.at[other, d], ybuf.at[other, d], ys.at[d, k], yr.at[d, k], dev(x, other, z))

    def xc(d, k):
        other = (x + k) % 4
        return rdma(ybuf.at[other, d], kbuf.at[d, mine], xs.at[d, k], xr.at[d, 4 - k], dev(other, y, z))

    def xw(d, k):
        other = (x + k) % 4
        where = kbuf.at[d, pl.ds(pl.multiple_of(other * PART, PART), PART)]
        return rdma(where, where, xs.at[d, k], xr.at[d, k], dev(other, y, z))

    def direct(k):
        return rdma(s_v, kbuf.at[0], ys.at[0, k], xr.at[0, 0], dev(x, (y + k) % 4, z))

    def y_send(d):
        zc(d).wait_recv()
        for k in (1, 3, 2):
            yc(d, k).start()

    def x_send(d):
        for k in (1, 3, 2):
            yw(d, k).wait_recv()
        for k in (1, 3, 2):
            xc(d, k).start()

    def x_wait(d):
        for k in (1, 3, 2):
            xw(d, k).wait_recv()
        kbuf[d, mine] = ybuf[x, d]

    for d in (1, 3, 2):
        zc(d).start()

    @pl.when(diag)
    def _():
        for k in (1, 3, 2):
            direct(k).start()
        kbuf[0] = s_v[...]

    gain_row = gain_v[...].reshape(1, D)
    normed = layer_norm(s_v[...], gain_row)
    spread = spread_matrix(0)(WIDE)
    dst, src = iota((WIDE, D), 0), iota((WIDE, D), 1)
    hit = (src == (dst // PAD) * HD + dst % PAD) & (dst % PAD < HD)
    spread_t = jnp.where(hit, 1.0, 0.0).astype(BF16)
    wkt[...] = mm_nt(spread_t, wk_v[...]).astype(BF16)
    wvp[...] = mm(wv_v[...], spread).astype(BF16)
    wqp = mm(wq_v[...], spread).astype(BF16)
    qb_row = qb_v[...].reshape(1, D)
    qb_hi = qb_row.astype(BF16)
    qb_rest = qb_row - qb_hi.astype(F32)
    qb_mid = qb_rest.astype(BF16)
    qb_lo = (qb_rest - qb_mid.astype(F32)).astype(BF16)
    qb_pad = mm(qb_hi, spread) + mm(qb_mid, spread) + mm(qb_lo, spread)
    query = (mm(normed, wqp) + qb_pad) * (1.0 / math.sqrt(HD))
    wide_lane = iota((ROWS, WIDE), 1) % PAD
    query = jnp.where((wide_lane == HD) | (wide_lane == HD + 1), 1.0, query)
    lane = iota((ROWS, LANES), 1)
    head_of = lane // PAD
    for h in range(HEADS):
        g, hh = divmod(h, 4)
        qm[h] = jnp.where(head_of == hh, query[:, g * LANES : (g + 1) * LANES], 0.0).astype(BF16)

    y_send(1)
    y_send(3)

    wop[...] = mm(spread_t, wo_v[...]).astype(BF16)
    wg = mm(wg_v[...], spread_matrix(col * 4)(LANES)).astype(BF16)
    gate_v[...] = jax.nn.sigmoid(mm(normed, wg))
    pick = (iota((D, OUTW), 0) == iota((D, OUTW), 1) + col * OUTW)
    cols_v[...] = mm(s_v[...], jnp.where(pick, 1.0, 0.0).astype(BF16))
    mrun[...] = jnp.full(mrun.shape, -1e30, F32)
    acc[...] = jnp.zeros(acc.shape, F32)

    y_send(2)
    x_send(1)

    @pl.when(jnp.logical_not(diag))
    def _():
        direct(1).wait_recv()

    def prepare(d):
        normed_k = layer_norm(kbuf[d], gain_row)
        keys = mm_nt(wkt[...], normed_k)
        flags = mask_v[chunk_cols(d)].reshape(1, ROWS).astype(F32) - 1.0
        feature = iota((WIDE, ROWS), 0) % PAD
        term = jnp.where(feature == HD, MASK_HI, jnp.where(feature == HD + 1, MASK_LO, 0.0))
        kt[...] = (keys + term * flags).astype(BF16)
        value = mm(normed_k, wvp[...])
        value = jnp.where(wide_lane == HD, 1.0, value)
        for h in range(HEADS):
            g, hh = divmod(h, 4)
            vm[g, hh * ROWS : (hh + 1) * ROWS] = jnp.where(
                head_of == hh, value[:, g * LANES : (g + 1) * LANES], 0.0
            ).astype(BF16)

    def group(d, g):
        key_tile = kt[pl.ds(pl.multiple_of(g * LANES, LANES), LANES)]
        old = mrun[g]
        new = old
        for hh in range(4):
            logits = mm(qm[g * 4 + hh], key_tile) + b_v[d, g * 4 + hh].astype(F32)
            peak = jnp.maximum(jnp.max(logits, axis=1, keepdims=True), old[:, hh * PAD : hh * PAD + 1])
            p4[:, hh * ROWS : (hh + 1) * ROWS] = jnp.exp(logits - peak).astype(BF16)
            new = jnp.where(head_of == hh, peak, new)
        total = acc[g] * jnp.exp(old - new) + mm(p4[...], vm[g])
        return total, new

    def run_group(d, g):
        total, new = group(d, g)
        acc[g] = total
        mrun[g] = new

    def chunk(d):
        bias_load(d).wait()
        prepare(d)

        def body(g, carry):
            run_group(d, g)
            return carry

        lax.fori_loop(0, GROUPS, body, 0)

    chunk(0)
    x_send(3)
    x_send(2)
    x_wait(1)
    chunk(1)
    x_wait(3)
    chunk(3)
    x_wait(2)
    bias_load(2).wait()
    prepare(2)

    sub = lane % PAD

    def finish(g):
        total, new = group(2, g)
        high = new.astype(BF16).astype(F32)
        low = (new - high).astype(BF16).astype(F32)
        total = total * jnp.exp(new - (high + low))
        return jnp.where(sub == HD + 1, high, jnp.where(sub == HD + 2, low, total))

    def pc(k):
        other = (x + k) % 4
        return rdma(part.at[other], got.at[4 - k], ps.at[k], pr.at[4 - k], dev(other, y, z))

    def pw(k):
        other = (x + k) % 4
        return rdma(got.at[k], got.at[k], ps.at[k], pr.at[k], dev(other, y, z))

    def send_body(k, carry):
        g = (x + k) % 4
        part[g] = finish(g)
        pc(k).start()
        return carry

    lax.fori_loop(1, 4, send_body, 0)
    got[0] = finish(x)
    for k in (1, 2, 3):
        pw(k).wait_recv()

    a, b = iota((LANES, LANES), 0), iota((LANES, LANES), 1)
    same = a // PAD == b // PAD
    pick_peak = jnp.where(same & ((a % PAD == HD + 1) | (a % PAD == HD + 2)), 1.0, 0.0).astype(BF16)
    pick_total = jnp.where(same & (a % PAD == HD), 1.0, 0.0).astype(BF16)
    peaks = [mm(got[k].astype(BF16), pick_peak) for k in range(4)]
    peak = jnp.maximum(jnp.maximum(peaks[0], peaks[1]), jnp.maximum(peaks[2], peaks[3]))
    total = sum(got[k] * jnp.exp(peaks[k] - peak) for k in range(4))
    total_hi = total.astype(BF16)
    total_lo = (total - total_hi.astype(F32)).astype(BF16)
    denom = mm(total_hi, pick_total) + mm(total_lo, pick_total)
    gated = jnp.where(sub < HD, gate_v[...] * (total / denom), 0.0).astype(BF16)
    gbuf[x] = gated

    def gc(k):
        return rdma(gbuf.at[x], gbuf.at[x], gs.at[k], gr.at[4 - k], dev((x + k) % 4, y, z))

    def gw(k):
        other = (x + k) % 4
        return rdma(gbuf.at[other], gbuf.at[other], gs.at[k], gr.at[k], dev(other, y, z))

    for k in (1, 3, 2):
        gc(k).start()
    for k in (1, 3, 2):
        gw(k).wait_recv()
    result = cols_v[...]
    for g in range(GROUPS):
        result = result + mm(gbuf[g], wop[g * LANES : (g + 1) * LANES])
    out[...] = result

    for d in (1, 3, 2):
        zc(d).wait_send()
        for k in (1, 2, 3):
            yc(d, k).wait_send()
            xc(d, k).wait_send()

    @pl.when(diag)
    def _():
        for k in (1, 2, 3):
            direct(k).wait_send()

    for k in (1, 2, 3):
        pc(k).wait_send()
        gc(k).wait_send()


def on_device(*args):
    hbm = pl.BlockSpec(memory_space=pltpu.MemorySpace.HBM)
    sem = pltpu.SemaphoreType.DMA
    vmem = pltpu.VMEM
    return pl.pallas_call(
        kernel,
        name="attention",
        out_shape=jax.ShapeDtypeStruct((ROWS, OUTW), F32),
        in_specs=[hbm] * 10,
        out_specs=pl.BlockSpec(memory_space=pltpu.VMEM),
        scratch_shapes=[
            vmem((ROWS, D), BF16),
            vmem((4, HEADS, ROWS, ROWS), BF16),
            vmem((4 * ROWS,), jnp.int32),
            vmem((D,), F32),
            vmem((D,), F32),
            vmem((D, D), BF16),
            vmem((D, D), BF16),
            vmem((D, D), BF16),
            vmem((D, D), BF16),
            vmem((D, OUTW), BF16),
            vmem((4, 4, PART, D), BF16),
            vmem((4, ROWS, D), BF16),
            vmem((HEADS, ROWS, LANES), BF16),
            vmem((WIDE, D), BF16),
            vmem((D, WIDE), BF16),
            vmem((WIDE, OUTW), BF16),
            vmem((ROWS, LANES), F32),
            vmem((ROWS, OUTW), F32),
            vmem((WIDE, ROWS), BF16),
            vmem((GROUPS, 4 * ROWS, LANES), BF16),
            vmem((ROWS, 4 * ROWS), BF16),
            vmem((GROUPS, ROWS, LANES), F32),
            vmem((GROUPS, ROWS, LANES), F32),
            vmem((GROUPS, ROWS, LANES), F32),
            vmem((4, ROWS, LANES), F32),
            vmem((4, ROWS, LANES), BF16),
            sem((9,)), sem((4,)), sem((4,)), sem((4,)),
            sem((4, 4)), sem((4, 4)), sem((4, 4)), sem((4, 4)),
            sem((4,)), sem((4,)), sem((4,)), sem((4,)),
        ],
        compiler_params=pltpu.CompilerParams(
            collective_id=0, has_side_effects=True, vmem_limit_bytes=58 * 1024 * 1024
        ),
    )(*args)


def solution(mesh):
    return jax.shard_map(
        on_device,
        mesh=mesh,
        in_specs=(
            P(("sample", "row"), None),
            P("sample", "row", "col"),
            P("sample"),
            P(),
            P(),
            P(),
            P(),
            P(),
            P(),
            P(None, "col"),
        ),
        out_specs=P(("sample", "row"), "col"),
        check_vma=False,
    )
```

time: 214 us -> 55.1 us (0.26)
  waiting for transfers between devices: 134 us -> 0 us
  Pallas kernels: 0 us -> 51.7 us
  blocking collectives: 24.2 us -> 0 us
  matrix products: 15.3 us -> 0 us
  between operations: 13.3 us -> 0.01 us
  other arithmetic: 11.2 us -> 0 us
  local copies, waits for them, and re-layouts: 14.4 us -> 3.26 us
    all_gather x3 -> x0, waiting for transfers between devices: 134 us -> none  [the longest x1 68.2 us: on_device(): lax.all_gather(key_local, 'row', axis=0, tiled=True)]
    pallas_call x0 -> x1, Pallas kernels: none -> 51.7 us  [on_device(): pl.pallas_call(kernel, name='attention', out_shape=jax.ShapeDtypeStruct((...]
    all_gather x2 -> x0, blocking collectives: 24.2 us -> none  [joined(): everything = jax.tree.map(lambda part: lax.all_gather(part, axis), array)]
    dot_general x6 -> x0, matrix products: 15.3 us -> none  [the longest x1 5.59 us: attend(): jnp.einsum('qhd,khd->hqk', query_heads, key_heads, preferred_element_type...]
    reduce_sum x3 -> x0, other arithmetic: 9.98 us -> none  [the longest x1 7.77 us: attend(): row_total = jnp.sum(exp_scores, axis=2)]
    dynamic_slice x13 -> x0, local copies, waits for them, and re-layouts: 5.9 us -> none  [the longest x9 3.68 us: lap(): return combine(so_far, jax.tree.map(lambda part: part[k], everything))]
    unnamed x13 -> x1, local copies, waits for them, and re-layouts: 5.86 us -> 1.63 us
  transfers between devices with their start and end apart: 3 -> 0, of which waited for: 2 -> 0; matrix products, arithmetic and copies ran while one was open for 6% -> 0% of each run, Pallas kernels for 0% -> 0%
where the time goes in v1:
time: 55.1 us; the launch traced here: 54.9 us
  Pallas kernels  51.7 us (94%)
  local copies, waits for them, and re-layouts  3.26 us (6%)
    pallas_call x1, Pallas kernels, on_device(): pl.pallas_call(kernel, name='attention', out_shape=jax.ShapeDtypeStruct((...  51.7 us
    pallas_call x1, local copies, waits for them, and re-layouts, on_device(): pl.pallas_call(kernel, name='attention', out_shape=jax.ShapeDtypeStruct((...  1.64 us
    unnamed x1, local copies, waits for them, and re-layouts  1.63 us

profile of v1, /device:TPU:8, one launch (start us, length us, event | category | flops | bytes accessed | tf_op | source)
XLA Modules:
  0.0 54.9 jit_solution(14217922880320752944)
XLA Ops:
  0.0 1.6 %copy.11.w_out = bf16[384,96]{1,0:T(8,128)(2,1)} copy(bf16[384,96]{0,1:T(8,128)(2,1)} %param.19) | data formatting | bytes 147456 | tf_op args[9]
  1.6 51.7 %attention.1 = f32[256,96]{1,0:T(8,128)} custom-call(bf16[256,384]{1,0:T(8,128)(2,1)} %single.1, bf16[16,256,1024]{2,1,0:T(8,128)(2,1)} %bias.1, s32[4096]{0:T(1024)} %mask.1, f32[384]{0:T(512)} %gain.1, bf16[384,384]{1,0:T(8,128)(2,1)} %w_query.1, f32[384]{0:T(512)} %q_bias.1, bf16[384,384]{1,0:T(8,128)(2,1)} %w_key.1, bf16[384,384]{1,0:T(8,128)(2,1)} %w_value.1, ...), custom_call_target="tpu_custom_call" | custom-call | tf_op jit(solution)/shard_map/attention/pallas_call | solution.py:329
  53.3 1.6 %copy.12 = f32[256,96]{0,1:T(8,128)} copy(f32[256,96]{1,0:T(8,128)} %attention.1) | data formatting | bytes 196608 | tf_op jit(solution)/shard_map/attention/pallas_call | solution.py:329

commit v2 on v1

--- a/solution.py
+++ b/solution.py
@@ -44,19 +44,22 @@
     return (centered * lax.rsqrt(var + 1e-05) * gain).astype(BF16)
 
 
-def spread_matrix(first):
-    def make(width):
-        src, dst = iota((D, width), 0), iota((D, width), 1)
-        hit = (src == (dst // PAD + first) * HD + dst % PAD) & (dst % PAD < HD)
-        return jnp.where(hit, 1.0, 0.0).astype(BF16)
-
-    return make
+def spread_matrix(width):
+    src, dst = iota((D, width), 0), iota((D, width), 1)
+    hit = (src == (dst // PAD) * HD + dst % PAD) & (dst % PAD < HD)
+    return jnp.where(hit, 1.0, 0.0).astype(BF16)
+
+
+def spread_rows(width, first):
+    dst, src = iota((width, D), 0), iota((width, D), 1)
+    hit = (src == (dst // PAD + first) * HD + dst % PAD) & (dst % PAD < HD)
+    return jnp.where(hit, 1.0, 0.0).astype(BF16)
 
 
 def kernel(
     single, bias, mask, gain, w_query, q_bias, w_key, w_value, w_gate, w_out, out,
     s_v, b_v, mask_v, gain_v, qb_v, wq_v, wk_v, wv_v, wg_v, wo_v,
-    ybuf, kbuf, qm, wkt, wvp, wop, gate_v, cols_v, kt, vm, p4, mrun, acc, part, got, gbuf,
+    ybuf, kbuf, qm, wkt, wvp, gate_v, cols_v, kt, vm, p4, mrep, mrun, acc, part, got, gbuf,
     lsem, bsem, zs, zr, ys, yr, xs, xr, ps, pr, gs, gr,
 ):
     col = lax.axis_index("col")
@@ -71,6 +74,13 @@
             src_ref=src, dst_ref=dst, send_sem=ssem, recv_sem=rsem,
             device_id=target, device_id_type=MESH,
         )
+
+    barrier = pltpu.get_barrier_semaphore()
+    peers = [dev((x + k) % 4, y, z) for k in (1, 2, 3)]
+    peers += [dev(x, (y + k) % 4, z) for k in (1, 2, 3)]
+    peers += [dev(x, y, (z + k) % 4) for k in (1, 2, 3)]
+    for peer in peers:
+        pl.semaphore_signal(barrier, inc=1, device_id=peer, device_id_type=MESH)
 
     tokens = 4 * ROWS
     loads = [
@@ -90,22 +100,11 @@
     def bias_load(d):
         return pltpu.make_async_copy(bias.at[:, :, chunk_cols(d)], b_v.at[d], bsem.at[d])
 
-    barrier = pltpu.get_barrier_semaphore()
-    peers = [dev((x + k) % 4, y, z) for k in (1, 2, 3)]
-    peers += [dev(x, (y + k) % 4, z) for k in (1, 2, 3)]
-    peers += [dev(x, y, (z + k) % 4) for k in (1, 2, 3)]
-    for peer in peers:
-        pl.semaphore_signal(barrier, inc=1, device_id=peer, device_id_type=MESH)
-    for d in order:
-        bias_load(d).start()
-
-    for load in loads:
-        load.wait()
     pl.semaphore_wait(barrier, len(peers))
 
     diag = x == y
     mine = pl.ds(pl.multiple_of(x * PART, PART), PART)
-    own = s_v.at[mine]
+    own = single.at[mine]
 
     def zc(d):
         return rdma(own, ybuf.at[y, d], zs.at[d], zr.at[d], dev(x, y, (z + 4 - d) % 4))
@@ -127,7 +126,7 @@
         return rdma(where, where, xs.at[d, k], xr.at[d, k], dev(other, y, z))
 
     def direct(k):
-        return rdma(s_v, kbuf.at[0], ys.at[0, k], xr.at[0, 0], dev(x, (y + k) % 4, z))
+        return rdma(single, kbuf.at[0], ys.at[0, k], xr.at[0, 0], dev(x, (y + k) % 4, z))
 
     def y_send(d):
         zc(d).wait_recv()
@@ -152,16 +151,20 @@
     def _():
         for k in (1, 3, 2):
             direct(k).start()
+
+    for d in order:
+        bias_load(d).start()
+    for load in loads:
+        load.wait()
+
+    @pl.when(diag)
+    def _():
         kbuf[0] = s_v[...]
 
     gain_row = gain_v[...].reshape(1, D)
     normed = layer_norm(s_v[...], gain_row)
-    spread = spread_matrix(0)(WIDE)
-    dst, src = iota((WIDE, D), 0), iota((WIDE, D), 1)
-    hit = (src == (dst // PAD) * HD + dst % PAD) & (dst % PAD < HD)
-    spread_t = jnp.where(hit, 1.0, 0.0).astype(BF16)
-    wkt[...] = mm_nt(spread_t, wk_v[...]).astype(BF16)
-    wvp[...] = mm(wv_v[...], spread).astype(BF16)
+    spread = spread_matrix(WIDE)
+    spread_t = spread_rows(WIDE, 0)
     wqp = mm(wq_v[...], spread).astype(BF16)
     qb_row = qb_v[...].reshape(1, D)
     qb_hi = qb_row.astype(BF16)
@@ -173,19 +176,21 @@
     wide_lane = iota((ROWS, WIDE), 1) % PAD
     query = jnp.where((wide_lane == HD) | (wide_lane == HD + 1), 1.0, query)
     lane = iota((ROWS, LANES), 1)
-    head_of = lane // PAD
+    head_of, sub = lane // PAD, lane % PAD
     for h in range(HEADS):
         g, hh = divmod(h, 4)
         qm[h] = jnp.where(head_of == hh, query[:, g * LANES : (g + 1) * LANES], 0.0).astype(BF16)
+    wkt[...] = mm_nt(spread_t, wk_v[...]).astype(BF16)
+    wvp[...] = mm(wv_v[...], spread).astype(BF16)
 
     y_send(1)
     y_send(3)
 
-    wop[...] = mm(spread_t, wo_v[...]).astype(BF16)
-    wg = mm(wg_v[...], spread_matrix(col * 4)(LANES)).astype(BF16)
-    gate_v[...] = jax.nn.sigmoid(mm(normed, wg))
-    pick = (iota((D, OUTW), 0) == iota((D, OUTW), 1) + col * OUTW)
-    cols_v[...] = mm(s_v[...], jnp.where(pick, 1.0, 0.0).astype(BF16))
+    wgt = mm_nt(spread_rows(LANES, col * 4), wg_v[...]).astype(BF16)
+    gate_v[...] = jax.nn.sigmoid(mm_nt(wgt, normed))
+    pick = iota((OUTW, D), 1) == iota((OUTW, D), 0) + col * OUTW
+    cols_v[...] = mm_nt(jnp.where(pick, 1.0, 0.0).astype(BF16), s_v[...])
+    mrep[...] = jnp.full(mrep.shape, -1e30, F32)
     mrun[...] = jnp.full(mrun.shape, -1e30, F32)
     acc[...] = jnp.zeros(acc.shape, F32)
 
@@ -216,17 +221,18 @@
         old = mrun[g]
         new = old
         for hh in range(4):
-            logits = mm(qm[g * 4 + hh], key_tile) + b_v[d, g * 4 + hh].astype(F32)
-            peak = jnp.maximum(jnp.max(logits, axis=1, keepdims=True), old[:, hh * PAD : hh * PAD + 1])
-            p4[:, hh * ROWS : (hh + 1) * ROWS] = jnp.exp(logits - peak).astype(BF16)
+            h = g * 4 + hh
+            logits = mm(qm[h], key_tile) + b_v[d, h].astype(F32)
+            peak = jnp.maximum(jnp.max(logits, axis=1, keepdims=True), mrep[h])
+            mrep[h] = peak
+            for j in (0, LANES):
+                p4[:, hh * ROWS + j : hh * ROWS + j + LANES] = jnp.exp(logits[:, j : j + LANES] - peak).astype(BF16)
             new = jnp.where(head_of == hh, peak, new)
         total = acc[g] * jnp.exp(old - new) + mm(p4[...], vm[g])
         return total, new
 
     def run_group(d, g):
-        total, new = group(d, g)
-        acc[g] = total
-        mrun[g] = new
+        acc[g], mrun[g] = group(d, g)
 
     def chunk(d):
         bias_load(d).wait()
@@ -249,46 +255,37 @@
     bias_load(2).wait()
     prepare(2)
 
-    sub = lane % PAD
+    def pc(k):
+        other = (x + k) % 4
+        return rdma(part.at[other], got.at[4 - k], ps.at[k], pr.at[4 - k], dev(other, y, z))
+
+    def pw(k):
+        other = (x + k) % 4
+        return rdma(got.at[k], got.at[k], ps.at[k], pr.at[k], dev(other, y, z))
 
     def finish(g):
         total, new = group(2, g)
-        high = new.astype(BF16).astype(F32)
-        low = (new - high).astype(BF16).astype(F32)
-        total = total * jnp.exp(new - (high + low))
-        return jnp.where(sub == HD + 1, high, jnp.where(sub == HD + 2, low, total))
-
-    def pc(k):
-        other = (x + k) % 4
-        return rdma(part.at[other], got.at[4 - k], ps.at[k], pr.at[4 - k], dev(other, y, z))
-
-    def pw(k):
-        other = (x + k) % 4
-        return rdma(got.at[k], got.at[k], ps.at[k], pr.at[k], dev(other, y, z))
+        part[g] = jnp.where(sub == HD + 1, new, total).T
 
     def send_body(k, carry):
-        g = (x + k) % 4
-        part[g] = finish(g)
+        finish((x + k) % 4)
         pc(k).start()
         return carry
 
     lax.fori_loop(1, 4, send_body, 0)
-    got[0] = finish(x)
+    finish(x)
     for k in (1, 2, 3):
         pw(k).wait_recv()
 
-    a, b = iota((LANES, LANES), 0), iota((LANES, LANES), 1)
-    same = a // PAD == b // PAD
-    pick_peak = jnp.where(same & ((a % PAD == HD + 1) | (a % PAD == HD + 2)), 1.0, 0.0).astype(BF16)
-    pick_total = jnp.where(same & (a % PAD == HD), 1.0, 0.0).astype(BF16)
-    peaks = [mm(got[k].astype(BF16), pick_peak) for k in range(4)]
-    peak = jnp.maximum(jnp.maximum(peaks[0], peaks[1]), jnp.maximum(peaks[2], peaks[3]))
-    total = sum(got[k] * jnp.exp(peaks[k] - peak) for k in range(4))
-    total_hi = total.astype(BF16)
-    total_lo = (total - total_hi.astype(F32)).astype(BF16)
-    denom = mm(total_hi, pick_total) + mm(total_lo, pick_total)
-    gated = jnp.where(sub < HD, gate_v[...] * (total / denom), 0.0).astype(BF16)
-    gbuf[x] = gated
+    rows = []
+    for hh in range(4):
+        parts = [part[x, hh * PAD : (hh + 1) * PAD]]
+        parts += [got[k, hh * PAD : (hh + 1) * PAD] for k in (1, 2, 3)]
+        peaks = [p[HD + 1 : HD + 2] for p in parts]
+        peak = jnp.maximum(jnp.maximum(peaks[0], peaks[1]), jnp.maximum(peaks[2], peaks[3]))
+        total = sum(p * jnp.exp(m - peak) for p, m in zip(parts, peaks))
+        rows.append(gate_v[hh * PAD : hh * PAD + HD] * (total[0:HD] / total[HD : HD + 1]))
+    gbuf[x] = jnp.concatenate(rows, axis=0).astype(BF16)
 
     def gc(k):
         return rdma(gbuf.at[x], gbuf.at[x], gs.at[k], gr.at[4 - k], dev((x + k) % 4, y, z))
@@ -301,10 +298,7 @@
         gc(k).start()
     for k in (1, 3, 2):
         gw(k).wait_recv()
-    result = cols_v[...]
-    for g in range(GROUPS):
-        result = result + mm(gbuf[g], wop[g * LANES : (g + 1) * LANES])
-    out[...] = result
+    out[...] = cols_v[...] + mm(wo_v[...], gbuf[...].reshape(D, ROWS))
 
     for d in (1, 3, 2):
         zc(d).wait_send()
@@ -323,13 +317,14 @@
 
 
 def on_device(*args):
+    *rest, w_out = args
     hbm = pl.BlockSpec(memory_space=pltpu.MemorySpace.HBM)
     sem = pltpu.SemaphoreType.DMA
     vmem = pltpu.VMEM
-    return pl.pallas_call(
+    result = pl.pallas_call(
         kernel,
         name="attention",
-        out_shape=jax.ShapeDtypeStruct((ROWS, OUTW), F32),
+        out_shape=jax.ShapeDtypeStruct((OUTW, ROWS), F32),
         in_specs=[hbm] * 10,
         out_specs=pl.BlockSpec(memory_space=pltpu.VMEM),
         scratch_shapes=[
@@ -342,23 +337,23 @@
             vmem((D, D), BF16),
             vmem((D, D), BF16),
             vmem((D, D), BF16),
-            vmem((D, OUTW), BF16),
+            vmem((OUTW, D), BF16),
             vmem((4, 4, PART, D), BF16),
             vmem((4, ROWS, D), BF16),
             vmem((HEADS, ROWS, LANES), BF16),
             vmem((WIDE, D), BF16),
             vmem((D, WIDE), BF16),
-            vmem((WIDE, OUTW), BF16),
-            vmem((ROWS, LANES), F32),
-            vmem((ROWS, OUTW), F32),
+            vmem((LANES, ROWS), F32),
+            vmem((OUTW, ROWS), F32),
             vmem((WIDE, ROWS), BF16),
             vmem((GROUPS, 4 * ROWS, LANES), BF16),
             vmem((ROWS, 4 * ROWS), BF16),
+            vmem((HEADS, ROWS, LANES), F32),
             vmem((GROUPS, ROWS, LANES), F32),
             vmem((GROUPS, ROWS, LANES), F32),
-            vmem((GROUPS, ROWS, LANES), F32),
-            vmem((4, ROWS, LANES), F32),
-            vmem((4, ROWS, LANES), BF16),
+            vmem((4, LANES, ROWS), F32),
+            vmem((4, LANES, ROWS), F32),
+            vmem((4, OUTW, ROWS), BF16),
             sem((9,)), sem((4,)), sem((4,)), sem((4,)),
             sem((4, 4)), sem((4, 4)), sem((4, 4)), sem((4, 4)),
             sem((4,)), sem((4,)), sem((4,)), sem((4,)),
@@ -366,7 +361,8 @@
         compiler_params=pltpu.CompilerParams(
             collective_id=0, has_side_effects=True, vmem_limit_bytes=58 * 1024 * 1024
         ),
-    )(*args)
+    )(*rest, w_out.T)
+    return result.T
 
 
 def solution(mesh):

time: 55.1 us -> 51 us (0.926)
  Pallas kernels: 51.7 us -> 49.3 us
  local copies, waits for them, and re-layouts: 3.26 us -> 1.54 us
    pallas_call x1, Pallas kernels: 51.7 us -> 49.3 us  [on_device(): pl.pallas_call(kernel, name='attention', out_shape=jax.ShapeDtypeStruct((...]
    pallas_call x1 -> x0, local copies, waits for them, and re-layouts: 1.64 us -> none  [on_device(): pl.pallas_call(kernel, name='attention', out_shape=jax.ShapeDtypeStruct((...]
where the time goes in v2:
time: 51 us; the launch traced here: 50.8 us
  Pallas kernels  49.3 us (97%)
  local copies, waits for them, and re-layouts  1.54 us (3%)
    pallas_call x1, Pallas kernels, on_device(): pl.pallas_call(kernel, name='attention', out_shape=jax.ShapeDtypeStruct((...  49.3 us
    unnamed x1, local copies, waits for them, and re-layouts  1.54 us

profile of v2, /device:TPU:8, one launch (start us, length us, event | category | flops | bytes accessed | tf_op | source)
XLA Modules:
  0.0 50.8 jit_solution(12384058428879765097)
XLA Ops:
  0.0 49.3 %attention.1 = f32[96,256]{1,0:T(8,128)} custom-call(bf16[256,384]{1,0:T(8,128)(2,1)} %single.1, bf16[16,256,1024]{2,1,0:T(8,128)(2,1)} %bias.1, s32[4096]{0:T(1024)} %mask.1, f32[384]{0:T(512)} %gain.1, bf16[384,384]{1,0:T(8,128)(2,1)} %w_query.1, f32[384]{0:T(512)} %q_bias.1, bf16[384,384]{1,0:T(8,128)(2,1)} %w_key.1, bf16[384,384]{1,0:T(8,128)(2,1)} %w_value.1, ...), custom_call_target="tpu_custom_call" | custom-call | tf_op jit(solution)/shard_map/attention/pallas_call | solution.py:324
  49.3 1.5 %copy.12 = f32[256,96]{0,1:T(8,128)} copy(f32[256,96]{0,1:T(8,128)} %bitcast.2) | data formatting | bytes 196608

commit v3 on v2

--- a/solution.py
+++ b/solution.py
@@ -17,6 +17,7 @@
 LANES = 128
 ROWS = 256
 PART = 64
+HALVES = 2
 OUTW = 96
 MESH = pl.DeviceIdType.MESH
 F32 = jnp.float32
@@ -58,9 +59,9 @@
 
 def kernel(
     single, bias, mask, gain, w_query, q_bias, w_key, w_value, w_gate, w_out, out,
-    s_v, b_v, mask_v, gain_v, qb_v, wq_v, wk_v, wv_v, wg_v, wo_v,
+    s_v, n_v, b_v, mask_v, gain_v, qb_v, wq_v, wk_v, wv_v, wg_v, wo_v,
     ybuf, kbuf, qm, wkt, wvp, gate_v, cols_v, kt, vm, p4, mrep, mrun, acc, part, got, gbuf,
-    lsem, bsem, zs, zr, ys, yr, xs, xr, ps, pr, gs, gr,
+    lsem, bsem, zs, zr, ys, yr, xs, xr, ps, pr, gs, gr, ds, dr, fs, fr,
 ):
     col = lax.axis_index("col")
     row = lax.axis_index("row")
@@ -100,69 +101,82 @@
     def bias_load(d):
         return pltpu.make_async_copy(bias.at[:, :, chunk_cols(d)], b_v.at[d], bsem.at[d])
 
+    for load in loads[:2]:
+        load.wait()
+    gain_row = gain_v[...].reshape(1, D)
+    n_v[...] = layer_norm(s_v[...], gain_row)
     pl.semaphore_wait(barrier, len(peers))
 
     diag = x == y
     mine = pl.ds(pl.multiple_of(x * PART, PART), PART)
-    own = single.at[mine]
-
-    def zc(d):
-        return rdma(own, ybuf.at[y, d], zs.at[d], zr.at[d], dev(x, y, (z + 4 - d) % 4))
-
-    def yc(d, k):
-        return rdma(ybuf.at[y, d], ybuf.at[y, d], ys.at[d, k], yr.at[d, 4 - k], dev(x, (y + k) % 4, z))
-
-    def yw(d, k):
+    own = n_v.at[mine]
+
+    def zc():
+        return rdma(own, ybuf.at[y], zs.at[0], zr.at[0], dev(x, y, (z + 2) % 4))
+
+    def yc(k):
+        return rdma(ybuf.at[y], ybuf.at[y], ys.at[k], yr.at[4 - k], dev(x, (y + k) % 4, z))
+
+    def yw(k):
         other = (y + k) % 4
-        return rdma(ybuf.at[other, d], ybuf.at[other, d], ys.at[d, k], yr.at[d, k], dev(x, other, z))
-
-    def xc(d, k):
+        return rdma(ybuf.at[other], ybuf.at[other], ys.at[k], yr.at[k], dev(x, other, z))
+
+    def xc(k):
         other = (x + k) % 4
-        return rdma(ybuf.at[other, d], kbuf.at[d, mine], xs.at[d, k], xr.at[d, 4 - k], dev(other, y, z))
-
-    def xw(d, k):
+        return rdma(ybuf.at[other], kbuf.at[2, mine], xs.at[k], xr.at[4 - k], dev(other, y, z))
+
+    def xw(k):
         other = (x + k) % 4
-        where = kbuf.at[d, pl.ds(pl.multiple_of(other * PART, PART), PART)]
-        return rdma(where, where, xs.at[d, k], xr.at[d, k], dev(other, y, z))
-
-    def direct(k):
-        return rdma(single, kbuf.at[0], ys.at[0, k], xr.at[0, 0], dev(x, (y + k) % 4, z))
-
-    def y_send(d):
-        zc(d).wait_recv()
+        where = kbuf.at[2, pl.ds(pl.multiple_of(other * PART, PART), PART)]
+        return rdma(where, where, xs.at[k], xr.at[k], dev(other, y, z))
+
+    def half(i):
+        return pl.ds(i * (ROWS // HALVES), ROWS // HALVES)
+
+    def direct(i, k):
+        return rdma(n_v.at[half(i)], kbuf.at[0, half(i)], ds.at[i, k], dr.at[i], dev(x, (y + k) % 4, z))
+
+    def onward(i, d):
+        return rdma(kbuf.at[0, half(i)], kbuf.at[d, half(i)], fs.at[i, d], fr.at[i, d], dev(x, y, (z + 4 - d) % 4))
+
+    def y_send():
+        zc().wait_recv()
         for k in (1, 3, 2):
-            yc(d, k).start()
-
-    def x_send(d):
+            yc(k).start()
+
+    def x_send():
         for k in (1, 3, 2):
-            yw(d, k).wait_recv()
+            yw(k).wait_recv()
         for k in (1, 3, 2):
-            xc(d, k).start()
-
-    def x_wait(d):
+            xc(k).start()
+
+    def x_wait():
         for k in (1, 3, 2):
-            xw(d, k).wait_recv()
-        kbuf[d, mine] = ybuf[x, d]
-
-    for d in (1, 3, 2):
-        zc(d).start()
+            xw(k).wait_recv()
+        kbuf[2, mine] = ybuf[x]
+
+    def onward_wait(d):
+        for i in range(HALVES):
+            onward(i, d).wait_recv()
+
+    zc().start()
 
     @pl.when(diag)
     def _():
-        for k in (1, 3, 2):
-            direct(k).start()
+        for i in range(HALVES):
+            for k in (1, 3, 2):
+                direct(i, k).start()
+        kbuf[0] = n_v[...]
+        for i in range(HALVES):
+            for d in (1, 3):
+                onward(i, d).start()
 
     for d in order:
         bias_load(d).start()
-    for load in loads:
+    for load in loads[2:]:
         load.wait()
 
-    @pl.when(diag)
-    def _():
-        kbuf[0] = s_v[...]
-
-    gain_row = gain_v[...].reshape(1, D)
-    normed = layer_norm(s_v[...], gain_row)
+    normed = n_v[...]
     spread = spread_matrix(WIDE)
     spread_t = spread_rows(WIDE, 0)
     wqp = mm(wq_v[...], spread).astype(BF16)
@@ -183,8 +197,14 @@
     wkt[...] = mm_nt(spread_t, wk_v[...]).astype(BF16)
     wvp[...] = mm(wv_v[...], spread).astype(BF16)
 
-    y_send(1)
-    y_send(3)
+    @pl.when(jnp.logical_not(diag))
+    def _():
+        for i in range(HALVES):
+            direct(i, 1).wait_recv()
+            for d in (1, 3):
+                onward(i, d).start()
+
+    y_send()
 
     wgt = mm_nt(spread_rows(LANES, col * 4), wg_v[...]).astype(BF16)
     gate_v[...] = jax.nn.sigmoid(mm_nt(wgt, normed))
@@ -194,15 +214,8 @@
     mrun[...] = jnp.full(mrun.shape, -1e30, F32)
     acc[...] = jnp.zeros(acc.shape, F32)
 
-    y_send(2)
-    x_send(1)
-
-    @pl.when(jnp.logical_not(diag))
-    def _():
-        direct(1).wait_recv()
-
     def prepare(d):
-        normed_k = layer_norm(kbuf[d], gain_row)
+        normed_k = kbuf[d]
         keys = mm_nt(wkt[...], normed_k)
         flags = mask_v[chunk_cols(d)].reshape(1, ROWS).astype(F32) - 1.0
         feature = iota((WIDE, ROWS), 0) % PAD
@@ -216,8 +229,8 @@
                 head_of == hh, value[:, g * LANES : (g + 1) * LANES], 0.0
             ).astype(BF16)
 
-    def group(d, g):
-        key_tile = kt[pl.ds(pl.multiple_of(g * LANES, LANES), LANES)]
+    def scores(d, g, turn):
+        key_tile = kt[g * LANES : (g + 1) * LANES] if isinstance(g, int) else kt[pl.ds(pl.multiple_of(g * LANES, LANES), LANES)]
         old = mrun[g]
         new = old
         for hh in range(4):
@@ -226,32 +239,31 @@
             peak = jnp.maximum(jnp.max(logits, axis=1, keepdims=True), mrep[h])
             mrep[h] = peak
             for j in (0, LANES):
-                p4[:, hh * ROWS + j : hh * ROWS + j + LANES] = jnp.exp(logits[:, j : j + LANES] - peak).astype(BF16)
+                p4[turn, :, hh * ROWS + j : hh * ROWS + j + LANES] = jnp.exp(logits[:, j : j + LANES] - peak).astype(BF16)
             new = jnp.where(head_of == hh, peak, new)
-        total = acc[g] * jnp.exp(old - new) + mm(p4[...], vm[g])
-        return total, new
-
-    def run_group(d, g):
-        acc[g], mrun[g] = group(d, g)
-
-    def chunk(d):
+        mrun[g] = new
+        acc[g] = acc[g] * jnp.exp(old - new)
+
+    def values(g, turn):
+        acc[g] += mm(p4[turn], vm[g])
+
+    def chunk(d, between=None):
         bias_load(d).wait()
         prepare(d)
-
-        def body(g, carry):
-            run_group(d, g)
-            return carry
-
-        lax.fori_loop(0, GROUPS, body, 0)
-
-    chunk(0)
-    x_send(3)
-    x_send(2)
-    x_wait(1)
+        for g in range(GROUPS):
+            scores(d, g, g % 2)
+            if g:
+                values(g - 1, (g - 1) % 2)
+            if g == 1 and between is not None:
+                between()
+        values(GROUPS - 1, (GROUPS - 1) % 2)
+
+    chunk(0, x_send)
+    onward_wait(1)
     chunk(1)
-    x_wait(3)
+    onward_wait(3)
     chunk(3)
-    x_wait(2)
+    x_wait()
     bias_load(2).wait()
     prepare(2)
 
@@ -264,27 +276,40 @@
         return rdma(got.at[k], got.at[k], ps.at[k], pr.at[k], dev(other, y, z))
 
     def finish(g):
-        total, new = group(2, g)
-        part[g] = jnp.where(sub == HD + 1, new, total).T
-
-    def send_body(k, carry):
+        whole = jnp.where(sub == HD + 1, mrun[g], acc[g]).T
+        heads = [whole[hh * PAD : (hh + 1) * PAD] for hh in range(4)]
+        for hh in range(4):
+            part[g, hh * HD : (hh + 1) * HD] = heads[hh][0:HD]
+        stats = [h[HD : HD + 1] for h in heads] + [h[HD + 1 : HD + 2] for h in heads]
+        part[g, OUTW : OUTW + 8] = jnp.concatenate(stats, axis=0)
+
+    def send(k):
         finish((x + k) % 4)
         pc(k).start()
-        return carry
-
-    lax.fori_loop(1, 4, send_body, 0)
+
+    for k in range(1, 5):
+        scores(2, (x + k) % 4, k % 2)
+        if k > 1:
+            values((x + k - 1) % 4, (k - 1) % 2)
+            send(k - 1)
+    values(x, 0)
     finish(x)
     for k in (1, 2, 3):
         pw(k).wait_recv()
 
+    parts = [part.at[x]] + [got.at[k] for k in (1, 2, 3)]
+    all_sums = [p[0:OUTW] for p in parts]
+    all_denoms = [p[OUTW : OUTW + 4] for p in parts]
+    all_peaks = [p[OUTW + 4 : OUTW + 8] for p in parts]
+    peak = jnp.maximum(jnp.maximum(all_peaks[0], all_peaks[1]), jnp.maximum(all_peaks[2], all_peaks[3]))
+    factors = [jnp.exp(p - peak) for p in all_peaks]
+    inverse = 1.0 / sum(f * n for f, n in zip(factors, all_denoms))
+    factors = [f * inverse for f in factors]
     rows = []
     for hh in range(4):
-        parts = [part[x, hh * PAD : (hh + 1) * PAD]]
-        parts += [got[k, hh * PAD : (hh + 1) * PAD] for k in (1, 2, 3)]
-        peaks = [p[HD + 1 : HD + 2] for p in parts]
-        peak = jnp.maximum(jnp.maximum(peaks[0], peaks[1]), jnp.maximum(peaks[2], peaks[3]))
-        total = sum(p * jnp.exp(m - peak) for p, m in zip(parts, peaks))
-        rows.append(gate_v[hh * PAD : hh * PAD + HD] * (total[0:HD] / total[HD : HD + 1]))
+        inside = slice(hh * HD, (hh + 1) * HD)
+        total = sum(s[inside] * f[hh : hh + 1] for s, f in zip(all_sums, factors))
+        rows.append(gate_v[hh * PAD : hh * PAD + HD] * total)
     gbuf[x] = jnp.concatenate(rows, axis=0).astype(BF16)
 
     def gc(k):
@@ -300,16 +325,19 @@
         gw(k).wait_recv()
     out[...] = cols_v[...] + mm(wo_v[...], gbuf[...].reshape(D, ROWS))
 
-    for d in (1, 3, 2):
-        zc(d).wait_send()
-        for k in (1, 2, 3):
-            yc(d, k).wait_send()
-            xc(d, k).wait_send()
+    zc().wait_send()
+    for k in (1, 2, 3):
+        yc(k).wait_send()
+        xc(k).wait_send()
+    for i in range(HALVES):
+        for d in (1, 3):
+            onward(i, d).wait_send()
 
     @pl.when(diag)
     def _():
-        for k in (1, 2, 3):
-            direct(k).wait_send()
+        for i in range(HALVES):
+            for k in (1, 2, 3):
+                direct(i, k).wait_send()
 
     for k in (1, 2, 3):
         pc(k).wait_send()
@@ -329,6 +357,7 @@
         out_specs=pl.BlockSpec(memory_space=pltpu.VMEM),
         scratch_shapes=[
             vmem((ROWS, D), BF16),
+            vmem((ROWS, D), BF16),
             vmem((4, HEADS, ROWS, ROWS), BF16),
             vmem((4 * ROWS,), jnp.int32),
             vmem((D,), F32),
@@ -338,7 +367,7 @@
             vmem((D, D), BF16),
             vmem((D, D), BF16),
             vmem((OUTW, D), BF16),
-            vmem((4, 4, PART, D), BF16),
+            vmem((4, PART, D), BF16),
             vmem((4, ROWS, D), BF16),
             vmem((HEADS, ROWS, LANES), BF16),
             vmem((WIDE, D), BF16),
@@ -347,16 +376,17 @@
             vmem((OUTW, ROWS), F32),
             vmem((WIDE, ROWS), BF16),
             vmem((GROUPS, 4 * ROWS, LANES), BF16),
-            vmem((ROWS, 4 * ROWS), BF16),
+            vmem((2, ROWS, 4 * ROWS), BF16),
             vmem((HEADS, ROWS, LANES), F32),
             vmem((GROUPS, ROWS, LANES), F32),
             vmem((GROUPS, ROWS, LANES), F32),
-            vmem((4, LANES, ROWS), F32),
-            vmem((4, LANES, ROWS), F32),
+            vmem((4, OUTW + 8, ROWS), F32),
+            vmem((4, OUTW + 8, ROWS), F32),
             vmem((4, OUTW, ROWS), BF16),
-            sem((9,)), sem((4,)), sem((4,)), sem((4,)),
-            sem((4, 4)), sem((4, 4)), sem((4, 4)), sem((4, 4)),
+            sem((9,)), sem((4,)), sem((1,)), sem((1,)),
             sem((4,)), sem((4,)), sem((4,)), sem((4,)),
+            sem((4,)), sem((4,)), sem((4,)), sem((4,)),
+            sem((HALVES, 4)), sem((HALVES,)), sem((HALVES, 4)), sem((HALVES, 4)),
         ],
         compiler_params=pltpu.CompilerParams(
             collective_id=0, has_side_effects=True, vmem_limit_bytes=58 * 1024 * 1024

time: 51 us -> 46 us (0.902)
  Pallas kernels: 49.3 us -> 44.3 us
    pallas_call x1, Pallas kernels: 49.3 us -> 44.3 us  [on_device(): pl.pallas_call(kernel, name='attention', out_shape=jax.ShapeDtypeStruct((...]
where the time goes in v3:
time: 46 us; the launch traced here: 45.8 us
  Pallas kernels  44.3 us (96%)
  local copies, waits for them, and re-layouts  1.54 us (3%)
    pallas_call x1, Pallas kernels, on_device(): pl.pallas_call(kernel, name='attention', out_shape=jax.ShapeDtypeStruct((...  44.3 us
    unnamed x1, local copies, waits for them, and re-layouts  1.54 us

profile of v3, /device:TPU:8, one launch (start us, length us, event | category | flops | bytes accessed | tf_op | source)
XLA Modules:
  0.0 45.8 jit_solution(7394527530634781427)
XLA Ops:
  0.0 44.3 %attention.1 = f32[96,256]{1,0:T(8,128)} custom-call(bf16[256,384]{1,0:T(8,128)(2,1)} %single.1, bf16[16,256,1024]{2,1,0:T(8,128)(2,1)} %bias.1, s32[4096]{0:T(1024)} %mask.1, f32[384]{0:T(512)} %gain.1, bf16[384,384]{1,0:T(8,128)(2,1)} %w_query.1, f32[384]{0:T(512)} %q_bias.1, bf16[384,384]{1,0:T(8,128)(2,1)} %w_key.1, bf16[384,384]{1,0:T(8,128)(2,1)} %w_value.1, ...), custom_call_target="tpu_custom_call" | custom-call | tf_op jit(solution)/shard_map/attention/pallas_call | solution.py:352
  44.3 1.5 %copy.12 = f32[256,96]{0,1:T(8,128)} copy(f32[256,96]{0,1:T(8,128)} %bitcast.2) | data formatting | bytes 196608

commit v4 on v3

--- a/solution.py
+++ b/solution.py
@@ -287,12 +287,13 @@
         finish((x + k) % 4)
         pc(k).start()
 
-    for k in range(1, 5):
-        scores(2, (x + k) % 4, k % 2)
-        if k > 1:
-            values((x + k - 1) % 4, (k - 1) % 2)
-            send(k - 1)
-    values(x, 0)
+    turns = (2, 1, 3, 0)
+    for i, k in enumerate(turns):
+        scores(2, (x + k) % 4, i % 2)
+        if i:
+            values((x + turns[i - 1]) % 4, (i - 1) % 2)
+            send(turns[i - 1])
+    values(x, 1)
     finish(x)
     for k in (1, 2, 3):
         pw(k).wait_recv()

time: 46 us -> 45.5 us (0.989)
  Pallas kernels: 44.3 us -> 43.8 us
    pallas_call x1, Pallas kernels: 44.3 us -> 43.8 us  [on_device(): pl.pallas_call(kernel, name='attention', out_shape=jax.ShapeDtypeStruct((...]
where the time goes in v4:
time: 45.5 us; the launch traced here: 45.3 us
  Pallas kernels  43.8 us (96%)
  local copies, waits for them, and re-layouts  1.54 us (3%)
    pallas_call x1, Pallas kernels, on_device(): pl.pallas_call(kernel, name='attention', out_shape=jax.ShapeDtypeStruct((...  43.8 us
    unnamed x1, local copies, waits for them, and re-layouts  1.54 us

profile of v4, /device:TPU:8, one launch (start us, length us, event | category | flops | bytes accessed | tf_op | source)
XLA Modules:
  0.0 45.3 jit_solution(17072103778704196998)
XLA Ops:
  0.0 43.8 %attention.1 = f32[96,256]{1,0:T(8,128)} custom-call(bf16[256,384]{1,0:T(8,128)(2,1)} %single.1, bf16[16,256,1024]{2,1,0:T(8,128)(2,1)} %bias.1, s32[4096]{0:T(1024)} %mask.1, f32[384]{0:T(512)} %gain.1, bf16[384,384]{1,0:T(8,128)(2,1)} %w_query.1, f32[384]{0:T(512)} %q_bias.1, bf16[384,384]{1,0:T(8,128)(2,1)} %w_key.1, bf16[384,384]{1,0:T(8,128)(2,1)} %w_value.1, ...), custom_call_target="tpu_custom_call" | custom-call | tf_op jit(solution)/shard_map/attention/pallas_call | solution.py:353
  43.8 1.5 %copy.12 = f32[256,96]{0,1:T(8,128)} copy(f32[256,96]{0,1:T(8,128)} %bitcast.2) | data formatting | bytes 196608

commit v5 on v4

--- a/solution.py
+++ b/solution.py
@@ -320,7 +320,7 @@
         other = (x + k) % 4
         return rdma(gbuf.at[other], gbuf.at[other], gs.at[k], gr.at[k], dev(other, y, z))
 
-    for k in (1, 3, 2):
+    for k in (2, 1, 3):
         gc(k).start()
     for k in (1, 3, 2):
         gw(k).wait_recv()

time: 45.5 us -> 44.9 us (0.987)
  Pallas kernels: 43.8 us -> 43.3 us
    pallas_call x1, Pallas kernels: 43.8 us -> 43.3 us  [on_device(): pl.pallas_call(kernel, name='attention', out_shape=jax.ShapeDtypeStruct((...]
where the time goes in v5:
time: 44.9 us; the launch traced here: 44.8 us
  Pallas kernels  43.3 us (96%)
  local copies, waits for them, and re-layouts  1.54 us (3%)
    pallas_call x1, Pallas kernels, on_device(): pl.pallas_call(kernel, name='attention', out_shape=jax.ShapeDtypeStruct((...  43.3 us
    unnamed x1, local copies, waits for them, and re-layouts  1.54 us

profile of v5, /device:TPU:8, one launch (start us, length us, event | category | flops | bytes accessed | tf_op | source)
XLA Modules:
  0.0 44.8 jit_solution(16731281710627231507)
XLA Ops:
  0.0 43.3 %attention.1 = f32[96,256]{1,0:T(8,128)} custom-call(bf16[256,384]{1,0:T(8,128)(2,1)} %single.1, bf16[16,256,1024]{2,1,0:T(8,128)(2,1)} %bias.1, s32[4096]{0:T(1024)} %mask.1, f32[384]{0:T(512)} %gain.1, bf16[384,384]{1,0:T(8,128)(2,1)} %w_query.1, f32[384]{0:T(512)} %q_bias.1, bf16[384,384]{1,0:T(8,128)(2,1)} %w_key.1, bf16[384,384]{1,0:T(8,128)(2,1)} %w_value.1, ...), custom_call_target="tpu_custom_call" | custom-call | tf_op jit(solution)/shard_map/attention/pallas_call | solution.py:353
  43.3 1.5 %copy.12 = f32[256,96]{0,1:T(8,128)} copy(f32[256,96]{0,1:T(8,128)} %bitcast.2) | data formatting | bytes 196608
